TPU v7x, 512 devices: a whole 4x4x16 slice. The times are simulated.
512 devices in a mesh: wide: 64 (over z_lo, x, core), narrow: 8 (over z_hi, y).
Axes of the slice: x: 4, y: 4, z: 16 (z_hi: 2, z_lo: 8; z = z_hi * 8 + z_lo), core: 2. Of those that a mesh axis runs over, the one named last changes fastest.
Arguments:
- tokens: bfloat16 [384, 12288], P('wide', 'narrow'), may hold values from -6 to 6
- up_weight: bfloat16 [12288, 49152], P('narrow', 'wide'), may hold values from -0.0546875 to 0.0546875
- down_weight: bfloat16 [49152, 12288], P('wide', 'narrow'), may hold values from -0.02734375 to 0.02734375
- partner: int32 [384], P('wide'), may hold values from 0 to 383, as said below
- spans: int32 [64, 2], P('wide'), may hold values from 1 to 5, as said below
Outputs:
- blended: bfloat16 [384, 12288], P('wide', 'narrow')
Inputs may be any that keep to these rules, and one draw needn't show every extreme that they name: Row r of block b has partner b' * 6 + j with some row j, where b' = b - 1 if r < spans[b, 0] and b > 0, b' = b + 1 if r >= spans[b, 1] and b < 63; every other token is its own partner. spans[b, 0] lies in 1 to 2 and spans[b, 1] in 4 to 5.
All inputs are finite; a program needn't handle non-finite values.
Results may differ from a plain program's by a relative error of at most 0.0049.
Values may be sent and summed in bfloat16 or wider, within the bound.
A program may use at most 64 MiB of HBM per device.

v0:
```python
import jax
import jax.numpy as jnp
from jax import lax
from jax.sharding import PartitionSpec as P


def with_halo(block, sides, width):
    for axis, dim in sides:
        count = lax.axis_size(axis)
        forward = [(i, i + 1) for i in range(count - 1)]
        backward = [(target, source) for source, target in forward]
        low = lax.ppermute(
            lax.slice_in_dim(block, block.shape[dim] - width, None, axis=dim), axis, forward
        )
        high = lax.ppermute(lax.slice_in_dim(block, 0, width, axis=dim), axis, backward)
        block = jnp.concatenate([low, block, high], axis=dim)
    return block


def blend_weights(spans, row_count):
    position = jnp.arange(row_count, dtype=jnp.int32)[None, :]
    lower_edge = spans[:, 0:1]
    upper_edge = spans[:, 1:2]
    from_left = jnp.where(
        position < lower_edge,
        jnp.float32(0.5)
        * (lower_edge - position).astype(jnp.float32)
        / lower_edge.astype(jnp.float32),
        jnp.float32(0.0),
    )
    from_right = jnp.where(
        position >= upper_edge,
        jnp.float32(0.5)
        * (position - upper_edge + 1).astype(jnp.float32)
        / (row_count - upper_edge).astype(jnp.float32),
        jnp.float32(0.0),
    )
    return (from_left + from_right).reshape(-1)


def body(tokens, up_weight, down_weight, partner, spans):
    row_count = tokens.shape[0]
    gathered = lax.all_gather(tokens, "wide", axis=0, tiled=True)
    preact_part = lax.psum_scatter(
        jnp.dot(gathered, up_weight, preferred_element_type=jnp.float32),
        "narrow",
        scatter_dimension=0,
        tiled=True,
    )
    hidden_part = jax.nn.gelu(preact_part, approximate=True).astype(jnp.bfloat16)
    hidden = lax.all_gather(hidden_part, "narrow", axis=0, tiled=True)
    summed = lax.psum_scatter(
        jnp.dot(hidden, down_weight, preferred_element_type=jnp.float32),
        "wide",
        scatter_dimension=0,
        tiled=True,
    )
    padded = with_halo(summed, (("wide", 0),), row_count)
    first_row = lax.axis_index("wide") * row_count
    local_index = partner - (first_row - row_count)
    share = blend_weights(spans, row_count)
    blended = summed + share[:, None] * (padded[local_index] - summed)
    return blended.astype(jnp.bfloat16)


def solution(mesh):
    placed = (
        P("wide", "narrow"),
        P("narrow", "wide"),
        P("wide", "narrow"),
        P("wide"),
        P("wide", None),
    )
    return jax.shard_map(
        body, mesh=mesh, in_specs=placed, out_specs=P("wide", "narrow"), check_vma=False
    )
```

profile of v0, /device:TPU:1, one launch (start us, length us, event | category | flops | bytes accessed | tf_op | source)
XLA Modules:
  0.0 629.0 jit_solution(12566293410756194784)
XLA Ops:
  6.5 0.7 all-gather.3.cloned.1.call-update
  7.3 0.0 reduce-scatter.4.cloned.1.call-start
  7.3 128.3 %all-gather.3.cloned.1.call-done = bf16[64,6,1536]{2,1,0:T(8,128)(2,1)} async-done(((bf16[1,6,1536]{2,1,0:T(8,128)(2,1)}), bf16[64,6,1536]{2,1,0:T(8,128)(2,1)}) %all-gather.3.cloned.1.call-update) | async-done | bytes 1179664 | tf_op jit(solution)/shard_map/all_gather | solution.py:43
  135.6 2.3 reshape.56
  137.9 3.8 fusion.11
  141.7 0.0 reduce-scatter.4.cloned.1.call-update
  141.7 116.2 %reduce-scatter.4.cloned.1.call-done = f32[48,768]{1,0:T(8,128)} async-done(((f32[384,768]{1,0:T(8,128)}), f32[48,768]{1,0:T(8,128)}) %reduce-scatter.4.cloned.1.call-update) | async-done | bytes 147472 | tf_op jit(solution)/shard_map/reduce_scatter | solution.py:44
  257.8 1.0 fusion.8
  258.8 59.9 %all_gather.7 = bf16[384,768]{1,0:T(8,128)(2,1)S(1)} all-gather(bf16[48,768]{1,0:T(8,128)(2,1)S(1)} %fusion.8), channel_id=1, replica_groups=mesh['wide'=64,'narrow'=8] {'narrow'}, dimensions={0}, use_global_device_ids=true | all-gather | bytes 663552 | tf_op jit(solution)/shard_map/all_gather | solution.py:51
  318.7 2.5 fusion.12
  321.2 233.7 %fusion = f32[8,1536]{1,0:T(8,128)S(1)} fusion(f32[384,1536]{1,0:T(8,128)} %fusion.12), kind=kCustom, calls=%all-reduce-scatter | all-reduce-scatter fusion | flops 786433 | bytes 2410496
  554.9 1.3 collective-permute-start.17
  556.2 1.3 collective-permute-start.10
  557.5 1.3 collective-permute-start.11
  558.8 1.3 collective-permute-start.12
  560.1 1.3 collective-permute-start.13
  561.4 10.6 %collective-permute-start.14 = (f32[8,1536]{1,0:T(8,128)S(1)}, f32[8,1536]{1,0:T(8,128)S(1)}, u32[]{:S(2)}, u32[]{:S(2)}) collective-permute-start(f32[8,1536]{1,0:T(8,128)S(1)} %fusion), channel_id=1, source_target_pairs={{0,104},{8,112},{16,120},{24,128},{32,136},{40,144},{48,152},{56,1... | collective-permute-start | bytes 147464
  572.0 1.7 collective-permute-start.15
  573.7 0.0 collective-permute-done.11
  573.7 1.3 collective-permute-start.16
  575.0 3.0 collective-permute-start.2
  578.0 0.0 collective-permute-done.13
  578.0 2.5 collective-permute-start.3
  580.6 3.4 collective-permute-start.4
  584.0 0.7 fusion.10
  584.7 0.0 collective-permute-done.15
  584.7 2.8 collective-permute-start.5
  587.4 0.0 collective-permute-done.16
  587.5 4.0 collective-permute-start.6
  591.4 0.0 collective-permute-done.2
  591.5 1.5 collective-permute-start.7
  592.9 0.0 collective-permute-done.3
  593.0 2.1 collective-permute-start.8
  595.1 0.0 collective-permute-done.4
  595.1 2.5 collective-permute-start.9
  598.9 1.3 dynamic-slice.4
  600.8 0.0 collective-permute-done.5
  600.9 0.6 copy-done.6
  601.4 0.0 copy-done.7
  601.4 0.0 copy-done.8
  601.5 0.6 copy-done.9
  602.1 9.9 %concatenate.4 = f32[134,1536]{1,0:T(8,128)S(1)} concatenate(f32[6,1536]{1,0:T(8,128)S(1)} %collective-permute-done.17, f32[8,1536]{1,0:T(8,128)} %copy-done.2, f32[8,1536]{1,0:T(8,128)} %copy-done.1, f32[8,1536]{1,0:T(8,128)S(1)} %collective-permute-done.14, f32[8,1536]{1,0:T(8,128)S(1)} %collective-permute-done.13, f32[8,1536]{1,0:T(8,128)S(1)} %collective-permute-done.12, ...), dimensions={0} | concatenate | bytes 1646592
  612.1 3.4 collective-permute-start
  615.4 1.9 collective-permute-start.1
  617.4 1.3 fusion.9
  618.6 2.2 collective-permute-done.1
  620.9 0.6 gather_fusion
  621.4 0.7 add_convert_fusion
  (35 shorter events, 0.1 us)
Async XLA Ops:
  6.5 312.2 %copy-start = (bf16[768,1536]{1,0:T(8,128)(2,1)S(1)}, bf16[768,1536]{1,0:T(8,128)(2,1)}, u32[]{:S(2)}) copy-start(bf16[768,1536]{1,0:T(8,128)(2,1)} %param.7) | copy-start | bytes 7077892
  6.5 129.1 %all-gather.3.cloned.1.call-start = ((), (), s32[]{:S(2)}) async-start(), calls=%async_computation.2 | async-start | bytes 1597440 | tf_op jit(solution)/shard_map/all_gather | solution.py:43
  7.3 250.6 %reduce-scatter.4.cloned.1.call-start = ((), (), s32[]{:S(2)}) async-start(), calls=%async_computation.1 | async-start | bytes 1327104 | tf_op jit(solution)/shard_map/reduce_scatter | solution.py:44
  321.2 250.8 %copy-start.11 = (s32[6]{0:T(128)S(1)}, s32[6]{0:T(128)}, u32[]{:S(2)}) copy-start(s32[6]{0:T(128)} %param.8) | copy-start | bytes 76
  321.2 262.8 %copy-start.10 = (s32[1,2]{1,0:T(1,128)S(1)}, s32[1,2]{1,0:T(1,128)}, u32[]{:S(2)}) copy-start(s32[1,2]{1,0:T(1,128)} %param.9) | copy-start | bytes 28
  554.9 6.5 %collective-permute-start.17 = (f32[6,1536]{1,0:T(8,128)S(1)}, f32[6,1536]{1,0:T(8,128)S(1)}, u32[]{:S(2)}, u32[]{:S(2)}) collective-permute-start(f32[6,1536]{1,0:T(8,128)S(1)} %slice.10), channel_id=1, source_target_pairs={{0,128},{8,136},{16,144},{24,152},{32,160},{40,168},{48,176},{56,1... | collective-permute-start | bytes 110600
  556.2 15.8 %collective-permute-start.10 = (f32[8,1536]{1,0:T(8,128)S(1)}, f32[8,1536]{1,0:T(8,128)S(1)}, u32[]{:S(2)}, u32[]{:S(2)}) collective-permute-start(f32[8,1536]{1,0:T(8,128)S(1)} %fusion), channel_id=1, source_target_pairs={{0,72},{8,80},{16,88},{24,96},{32,104},{40,112},{48,120},{56,128},... | collective-permute-start | bytes 147464
  557.5 16.2 %collective-permute-start.11 = (f32[8,1536]{1,0:T(8,128)S(1)}, f32[8,1536]{1,0:T(8,128)S(1)}, u32[]{:S(2)}, u32[]{:S(2)}) collective-permute-start(f32[8,1536]{1,0:T(8,128)S(1)} %fusion), channel_id=1, source_target_pairs={{0,80},{8,88},{16,96},{24,104},{32,112},{40,120},{48,128},{56,136}... | collective-permute-start | bytes 147464
  558.8 16.2 %collective-permute-start.12 = (f32[8,1536]{1,0:T(8,128)S(1)}, f32[8,1536]{1,0:T(8,128)S(1)}, u32[]{:S(2)}, u32[]{:S(2)}) collective-permute-start(f32[8,1536]{1,0:T(8,128)S(1)} %fusion), channel_id=1, source_target_pairs={{0,88},{8,96},{16,104},{24,112},{32,120},{40,128},{48,136},{56,144... | collective-permute-start | bytes 147464
  560.1 17.9 %collective-permute-start.13 = (f32[8,1536]{1,0:T(8,128)S(1)}, f32[8,1536]{1,0:T(8,128)S(1)}, u32[]{:S(2)}, u32[]{:S(2)}) collective-permute-start(f32[8,1536]{1,0:T(8,128)S(1)} %fusion), channel_id=1, source_target_pairs={{0,96},{8,104},{16,112},{24,120},{32,128},{40,136},{48,144},{56,15... | collective-permute-start | bytes 147464
  561.4 19.1 %collective-permute-start.14 = (f32[8,1536]{1,0:T(8,128)S(1)}, f32[8,1536]{1,0:T(8,128)S(1)}, u32[]{:S(2)}, u32[]{:S(2)}) collective-permute-start(f32[8,1536]{1,0:T(8,128)S(1)} %fusion), channel_id=1, source_target_pairs={{0,104},{8,112},{16,120},{24,128},{32,136},{40,144},{48,152},{56,1... | collective-permute-start | bytes 147464
  572.0 12.6 %collective-permute-start.15 = (f32[8,1536]{1,0:T(8,128)S(1)}, f32[8,1536]{1,0:T(8,128)S(1)}, u32[]{:S(2)}, u32[]{:S(2)}) collective-permute-start(f32[8,1536]{1,0:T(8,128)S(1)} %fusion), channel_id=1, source_target_pairs={{0,112},{8,120},{16,128},{24,136},{32,144},{40,152},{48,160},{56,1... | collective-permute-start | bytes 147464
  573.7 13.7 %collective-permute-start.16 = (f32[8,1536]{1,0:T(8,128)S(1)}, f32[8,1536]{1,0:T(8,128)S(1)}, u32[]{:S(2)}, u32[]{:S(2)}) collective-permute-start(f32[8,1536]{1,0:T(8,128)S(1)} %fusion), channel_id=1, source_target_pairs={{0,120},{8,128},{16,136},{24,144},{32,152},{40,160},{48,168},{56,1... | collective-permute-start | bytes 147464
  575.0 16.4 %collective-permute-start.2 = (f32[8,1536]{1,0:T(8,128)S(1)}, f32[8,1536]{1,0:T(8,128)S(1)}, u32[]{:S(2)}, u32[]{:S(2)}) collective-permute-start(f32[8,1536]{1,0:T(8,128)S(1)} %fusion), channel_id=1, source_target_pairs={{0,8},{8,16},{16,24},{24,32},{32,40},{40,48},{48,56},{56,64},{64,7... | collective-permute-start | bytes 147464
  578.0 14.9 %collective-permute-start.3 = (f32[8,1536]{1,0:T(8,128)S(1)}, f32[8,1536]{1,0:T(8,128)S(1)}, u32[]{:S(2)}, u32[]{:S(2)}) collective-permute-start(f32[8,1536]{1,0:T(8,128)S(1)} %fusion), channel_id=1, source_target_pairs={{0,16},{8,24},{16,32},{24,40},{32,48},{40,56},{48,64},{56,72},{64,... | collective-permute-start | bytes 147464
  580.6 14.5 %collective-permute-start.4 = (f32[8,1536]{1,0:T(8,128)S(1)}, f32[8,1536]{1,0:T(8,128)S(1)}, u32[]{:S(2)}, u32[]{:S(2)}) collective-permute-start(f32[8,1536]{1,0:T(8,128)S(1)} %fusion), channel_id=1, source_target_pairs={{0,24},{8,32},{16,40},{24,48},{32,56},{40,64},{48,72},{56,80},{64,... | collective-permute-start | bytes 147464
  584.7 10.4 %copy-start.1 = (f32[8,1536]{1,0:T(8,128)}, f32[8,1536]{1,0:T(8,128)S(1)}, u32[]{:S(2)}) copy-start(f32[8,1536]{1,0:T(8,128)S(1)} %collective-permute-done.15) | copy-start | bytes 147460
  584.7 16.1 %collective-permute-start.5 = (f32[8,1536]{1,0:T(8,128)S(1)}, f32[8,1536]{1,0:T(8,128)S(1)}, u32[]{:S(2)}, u32[]{:S(2)}) collective-permute-start(f32[8,1536]{1,0:T(8,128)S(1)} %fusion), channel_id=1, source_target_pairs={{0,32},{8,40},{16,48},{24,56},{32,64},{40,72},{48,80},{56,88},{64,... | collective-permute-start | bytes 147464
  587.4 10.1 %copy-start.2 = (f32[8,1536]{1,0:T(8,128)}, f32[8,1536]{1,0:T(8,128)S(1)}, u32[]{:S(2)}) copy-start(f32[8,1536]{1,0:T(8,128)S(1)} %collective-permute-done.16) | copy-start | bytes 147460
  587.5 13.4 %collective-permute-start.6 = (f32[8,1536]{1,0:T(8,128)S(1)}, f32[8,1536]{1,0:T(8,128)S(1)}, u32[]{:S(2)}, u32[]{:S(2)}) collective-permute-start(f32[8,1536]{1,0:T(8,128)S(1)} %fusion), channel_id=1, source_target_pairs={{0,40},{8,48},{16,56},{24,64},{32,72},{40,80},{48,88},{56,96},{64,... | collective-permute-start | bytes 147464
  591.5 6.1 copy-start.3
  591.5 9.4 %collective-permute-start.7 = (f32[8,1536]{1,0:T(8,128)S(1)}, f32[8,1536]{1,0:T(8,128)S(1)}, u32[]{:S(2)}, u32[]{:S(2)}) collective-permute-start(f32[8,1536]{1,0:T(8,128)S(1)} %fusion), channel_id=1, source_target_pairs={{0,48},{8,56},{16,64},{24,72},{32,80},{40,88},{48,96},{56,104},{64... | collective-permute-start | bytes 147464
  593.0 4.6 copy-start.4
  593.0 7.9 %collective-permute-start.8 = (f32[8,1536]{1,0:T(8,128)S(1)}, f32[8,1536]{1,0:T(8,128)S(1)}, u32[]{:S(2)}, u32[]{:S(2)}) collective-permute-start(f32[8,1536]{1,0:T(8,128)S(1)} %fusion), channel_id=1, source_target_pairs={{0,56},{8,64},{16,72},{24,80},{32,88},{40,96},{48,104},{56,112},{6... | collective-permute-start | bytes 147464
  595.1 2.5 copy-start.5
  595.1 7.0 %collective-permute-start.9 = (f32[8,1536]{1,0:T(8,128)S(1)}, f32[8,1536]{1,0:T(8,128)}, u32[]{:S(2)}, u32[]{:S(2)}) collective-permute-start(f32[8,1536]{1,0:T(8,128)S(1)} %fusion), channel_id=1, source_target_pairs={{0,64},{8,72},{16,80},{24,88},{32,96},{40,104},{48,112},{56,120},{... | collective-permute-start | bytes 147464
  600.8 0.6 copy-start.6
  600.8 0.6 copy-start.7
  600.8 0.6 copy-start.8
  601.5 0.6 copy-start.9
  612.1 6.6 %collective-permute-start = (f32[6,1536]{1,0:T(8,128)S(1)}, f32[6,1536]{1,0:T(8,128)S(1)}, u32[]{:S(2)}, u32[]{:S(2)}) collective-permute-start(f32[6,1536]{1,0:T(8,128)S(1)} %constant_dynamic-slice_fusion), channel_id=1, source_target_pairs={{0,8},{8,16},{16,24},{24,32},{32,40},{40,48},{48,56},{56,64},{64,7... | collective-permute-start | bytes 110600 | tf_op jit(solution)/shard_map/ppermute | solution.py:12
  615.4 5.4 collective-permute-start.1
Sparse Core Ops, SparseCore 0:
  9.5 126.0 all-gather.2
  141.8 115.9 reduce-scatter.3
where the time goes:
time: 630 us; the launch traced here: 629 us
  blocking collectives  294 us (47%)
  waiting for transfers between devices  247 us (39%)
  starting transfers between devices  47 us (7%)
  local copies, waits for them, and re-layouts  16 us (3%)
  between operations  15.7 us (2%)
    unnamed x1, blocking collectives  234 us
    all_gather x1, waiting for transfers between devices, body(): gathered = lax.all_gather(tokens, 'wide', axis=0, tiled=True)  128 us
    reduce_scatter x1, waiting for transfers between devices, body(): lax.psum_scatter(jnp.dot(gathered, up_weight, preferred_element_type=jnp....  116 us
    all_gather x1, blocking collectives, body(): hidden = lax.all_gather(hidden_part, 'narrow', axis=0, tiled=True)  59.9 us
    unnamed x16, starting transfers between devices  41.7 us
    unnamed x29, local copies, waits for them, and re-layouts  14.8 us
  transfers between devices with their start and end apart: 20, of which 3 were waited for; matrix products, arithmetic and copies ran while one was open for 1% of the time, Pallas kernels for 0%

commit v1 on v0

v1 whole, which is shorter than its diff:
```python
import jax
import jax.numpy as jnp
from jax import lax
from jax.experimental import pallas as pl
from jax.experimental.pallas import tpu as pltpu
from jax.sharding import PartitionSpec as P

MESH = pl.DeviceIdType.MESH
BF16 = jnp.bfloat16
F32 = jnp.float32

NZ, NX, NC, NY = 8, 4, 2, 4
ROWS = 6
SLAB = NZ * ROWS
GROUPS = NC * NX
TOKENS = GROUPS * SLAB
DM = 1536
FF = 768
GA = 2
WA = DM // GA
KB = 3
WB = FF // KB
JD = 3
WD = DM // JD
YR = TOKENS // NY


def steps(values, size, count):
    total = jnp.zeros_like(values)
    for k in range(1, count):
        total = total + jnp.where(values >= size * k, 1, 0)
    return total


def onehot(condition):
    return jnp.where(condition, 1.0, 0.0).astype(BF16)


def dot(a, b):
    return jnp.dot(a, b, preferred_element_type=F32)


def token_of(place):
    group = steps(place, SLAB, GROUPS)
    inside = place - SLAB * group
    z = steps(inside, ROWS, NZ)
    core = jnp.where(group >= NX, 1, 0)
    block = (z * NX + (group - NX * core)) * NC + core
    return block, ROWS * block + inside - ROWS * z


def kernel(
    tok_ref, partner_ref, spans_ref, up_hbm, down_hbm, out_ref,
    up, down, zbuf, g0, g1, p1, mix, ysend, yrecv, ysum, hsend, hrecv, hid, p2,
    csend, crecv, xsend, xrecv, xown, zsend, zrecv,
    wsem, az_s, az_r, ax_s, ax_r, ac_s, ac_r, by_s, by_r, bh_s, bh_r, cy_s, cy_r,
    dc_s, dc_r, dx_s, dx_r, dz_s, dz_r,
):
    w = lax.axis_index("wide")
    n = lax.axis_index("narrow")
    z, x, c = w // 8, (w // 2) % 4, w % 2
    half, y = n // 4, n % 4
    g = (g0, g1)

    def z_peer(d):
        return (((z + d) % NZ * NX + x) * NC + c, n)

    def x_peer(d):
        return ((z * NX + (x + d) % NX) * NC + c, n)

    def y_peer(d):
        return (w, half * NY + (y + d) % NY)

    core_peer = ((z * NX + x) * NC + 1 - c, n)
    half_peer = (w, (1 - half) * NY + y)

    def remote(src, dst, send, recv, peer):
        return pltpu.make_async_remote_copy(
            src_ref=src, dst_ref=dst, send_sem=send, recv_sem=recv, device_id=peer, device_id_type=MESH
        )

    sent = []

    def start(copy):
        copy.start()
        sent.append(copy)

    up_copy = pltpu.make_async_copy(up_hbm, up, wsem.at[0])
    down_copy = pltpu.make_async_copy(down_hbm, down, wsem.at[1])
    up_copy.start()
    down_copy.start()

    barrier = pltpu.get_barrier_semaphore()
    peers = [half_peer]
    peers += [z_peer(d) for d in range(1, NZ)]
    peers += [y_peer(d) for d in range(1, NY)]
    peers += [x_peer(d) for d in range(1, NX)]
    peers += [core_peer]
    for peer in peers:
        pl.semaphore_signal(barrier, inc=1, device_id=peer, device_id_type=MESH)

    tokens = tok_ref[...].astype(F32)
    tokens = jnp.concatenate([tokens, jnp.zeros((2, DM), F32)], axis=0)
    for i in range(GA):
        left = tokens[:, i * WA : i * WA + WA // 2]
        right = tokens[:, i * WA + WA // 2 : (i + 1) * WA]
        plane = jnp.concatenate([left, right], axis=0)
        if i == GA - 1:
            row = lax.broadcasted_iota(jnp.int32, (16, WA // 2), 0)
            lane = lax.broadcasted_iota(jnp.int32, (16, WA // 2), 1)
            lower = jnp.full((16, WA // 2), spans_ref[0, 0], jnp.int32).astype(F32)
            upper = jnp.full((16, WA // 2), spans_ref[0, 1], jnp.int32).astype(F32)
            for r in range(ROWS):
                relative = partner_ref[r] - ROWS * (w - 1)
                relative = jnp.full((16, WA // 2), relative, jnp.int32).astype(F32)
                share = jnp.where(lower > r, 0.5 * (lower - r) / lower, 0.0) + jnp.where(
                    upper <= r, 0.5 * (r - upper + 1.0) / (ROWS - upper), 0.0
                )
                here = row == ROWS + r // 3
                plane = jnp.where(here & (lane == 128 * (r % 3)), relative, plane)
                plane = jnp.where(here & (lane == 128 * (r % 3) + 1), share, plane)
        zbuf[i, z] = plane.astype(BF16)

    pl.semaphore_wait(barrier, len(peers))

    for i in range(GA):
        for d in (7, 1, 6, 2, 5, 3, 4):
            mine = zbuf.at[i, z]
            start(remote(mine, mine, az_s.at[i, d], az_r.at[i, d], z_peer(d)))

    m_at = lax.broadcasted_iota(jnp.int32, (SLAB, NZ * 16), 0)
    q_at = lax.broadcasted_iota(jnp.int32, (SLAB, NZ * 16), 1)
    m_z = steps(m_at, ROWS, NZ)
    m_r = m_at - ROWS * m_z
    pick_left = onehot(q_at == 16 * m_z + m_r)
    pick_right = onehot(q_at == 16 * m_z + m_r + 8)
    m_third = jnp.where(m_r >= 3, 1, 0)
    pick_info = [
        onehot((q_at == 16 * m_z + ROWS + m_third) & (m_r - 3 * m_third == t)) for t in range(3)
    ]

    group = c * NX + x
    for i in range(GA):
        for d in range(1, NZ):
            slot = zbuf.at[i, (z + NZ - d) % NZ]
            remote(slot, slot, az_s.at[i, d], az_r.at[i, d], z_peer(d)).wait_recv()
        planes = zbuf[i].reshape(NZ * 16, WA // 2)
        g[i][group, :, 0 : WA // 2] = dot(pick_left, planes).astype(BF16)
        g[i][group, :, WA // 2 : WA] = dot(pick_right, planes).astype(BF16)
        if i == GA - 1:
            info = dot(pick_info[0], planes[:, 0:128])
            info = info + dot(pick_info[1], planes[:, 128:256])
            info = info + dot(pick_info[2], planes[:, 256:384])
            g[i][group, :, WA : WA + 128] = info.astype(BF16)
        slab = g[i].at[group]
        for d in (2, 1, 3):
            start(remote(slab, slab, ax_s.at[i, d], ax_r.at[i, d], x_peer(d)))
        start(remote(slab, slab, ac_s.at[i, 0], ac_r.at[i, 0], core_peer))

    up_copy.wait()
    for i in range(GA):
        for d in (1, 3, 2):
            slab = g[i].at[c * NX + (x + NX - d) % NX]
            remote(slab, slab, ax_s.at[i, d], ax_r.at[i, d], x_peer(d)).wait_recv()
            start(remote(slab, slab, ac_s.at[i, d], ac_r.at[i, d], core_peer))
        for d in (0, 1, 3, 2):
            slab = g[i].at[(1 - c) * NX + (x + NX - d) % NX]
            remote(slab, slab, ac_s.at[i, d], ac_r.at[i, d], core_peer).wait_recv()
        a = g[i][:, :, 0:WA].reshape(TOKENS, WA)
        rows = pl.ds(i * WA, WA)
        for k in range(KB):
            part = dot(a, up[rows, k * WB : (k + 1) * WB]).reshape(NY, YR, WB)
            if i == 0:
                p1[k] = part
            else:
                part = part + p1[k]
                p1[k] = part
                ysend[k] = part.astype(BF16)
                for d in (2, 1, 3):
                    start(
                        remote(
                            ysend.at[k, (y + d) % NY], yrecv.at[k, d], by_s.at[k, d], by_r.at[k, d], y_peer(d)
                        )
                    )

    info = g1[:, :, WA : WA + 128].reshape(TOKENS, 128).astype(F32)
    block, _ = token_of(lax.broadcasted_iota(jnp.int32, (TOKENS, 1), 0))
    partner = (ROWS * (block - 1)).astype(F32) + info[:, 0:1]
    share = info[:, 1:2]
    _, token = token_of(lax.broadcasted_iota(jnp.int32, (1, TOKENS), 1))
    at = lax.broadcasted_iota(jnp.int32, (TOKENS, TOKENS), 0)
    to = lax.broadcasted_iota(jnp.int32, (TOKENS, TOKENS), 1)
    matrix = jnp.where(at == to, 1.0 - share, 0.0) + jnp.where(token.astype(F32) == partner, share, 0.0)
    mix[...] = matrix.astype(BF16)

    for k in range(KB):
        total = p1[k, y]
        for d in (1, 3, 2):
            remote(yrecv.at[k, d], yrecv.at[k, d], by_s.at[k, d], by_r.at[k, d], y_peer(d)).wait_recv()
            total = total + yrecv[k, d].astype(F32)
        ysum[k] = total
        hsend[k] = total.astype(BF16)
        start(remote(hsend.at[k], hrecv.at[k], bh_s.at[k], bh_r.at[k], half_peer))
    for k in range(KB):
        remote(hsend.at[k], hrecv.at[k], bh_s.at[k], bh_r.at[k], half_peer).wait_recv()
        preact = ysum[k] + hrecv[k].astype(F32)
        hid[k, y] = jax.nn.gelu(preact, approximate=True).astype(BF16)
        mine = hid.at[k, y]
        for d in (2, 1, 3):
            start(remote(mine, mine, cy_s.at[k, d], cy_r.at[k, d], y_peer(d)))

    down_copy.wait()
    for k in range(KB):
        for d in (1, 3, 2):
            slot = hid.at[k, (y + NY - d) % NY]
            remote(slot, slot, cy_s.at[k, d], cy_r.at[k, d], y_peer(d)).wait_recv()
        hidden = dot(mix[...], hid[k].reshape(TOKENS, WB)).astype(BF16)
        rows = pl.ds(k * WB, WB)
        if k < KB - 1:
            part = dot(hidden, down[rows, :])
            if k > 0:
                part = part + p2[...].reshape(TOKENS, DM)
            p2[...] = part.reshape(NC, TOKENS // NC, DM)
        else:
            for j in range(JD):
                cols = pl.ds(j * WD, WD)
                part = dot(hidden, down[rows, j * WD : (j + 1) * WD])
                p2[:, :, cols] = p2[:, :, cols] + part.reshape(NC, TOKENS // NC, WD)
                csend[j] = p2[1 - c, :, cols].astype(BF16)
                start(remote(csend.at[j], crecv.at[j], dc_s.at[j], dc_r.at[j], core_peer))

    for j in range(JD):
        remote(csend.at[j], crecv.at[j], dc_s.at[j], dc_r.at[j], core_peer).wait_recv()
        total = p2[c, :, pl.ds(j * WD, WD)] + crecv[j].astype(F32)
        total = total.reshape(NX, SLAB, WD)
        xown[j] = total
        xsend[j] = total.astype(BF16)
        for d in (2, 1, 3):
            start(remote(xsend.at[j, (x + d) % NX], xrecv.at[j, d], dx_s.at[j, d], dx_r.at[j, d], x_peer(d)))
    p_at = lax.broadcasted_iota(jnp.int32, (NZ * 16, SLAB), 0)
    s_at = lax.broadcasted_iota(jnp.int32, (NZ * 16, SLAB), 1)
    p_z = steps(p_at, 16, NZ)
    p_r = p_at - 16 * p_z
    put_left = onehot((s_at == ROWS * p_z + p_r) & (p_r < ROWS))
    put_right = onehot((s_at == ROWS * p_z + p_r - 8) & (p_r >= 8) & (p_r < 8 + ROWS))
    for j in range(JD):
        total = xown[j, x]
        for d in (1, 3, 2):
            remote(xrecv.at[j, d], xrecv.at[j, d], dx_s.at[j, d], dx_r.at[j, d], x_peer(d)).wait_recv()
            total = total + xrecv[j, d].astype(F32)
        total = total.astype(BF16)
        planes = dot(put_left, total[:, 0 : WD // 2]) + dot(put_right, total[:, WD // 2 : WD])
        zsend[j] = planes.reshape(NZ, 16, WD // 2).astype(BF16)
        for d in (7, 1, 6, 2, 5, 3, 4):
            start(remote(zsend.at[j, (z + d) % NZ], zrecv.at[j, d], dz_s.at[j, d], dz_r.at[j, d], z_peer(d)))
    for j in range(JD):
        total = zsend[j, z].astype(F32)
        for d in (1, 7, 2, 6, 3, 5, 4):
            remote(zrecv.at[j, d], zrecv.at[j, d], dz_s.at[j, d], dz_r.at[j, d], z_peer(d)).wait_recv()
            total = total + zrecv[j, d].astype(F32)
        out_ref[:, j * WD : j * WD + WD // 2] = total[0:ROWS].astype(BF16)
        out_ref[:, j * WD + WD // 2 : (j + 1) * WD] = total[8 : 8 + ROWS].astype(BF16)

    for copy in sent:
        copy.wait_send()


def body(tokens, up_weight, down_weight, partner, spans):
    dma = pltpu.SemaphoreType.DMA
    vmem = pltpu.VMEM
    return pl.pallas_call(
        kernel,
        out_shape=jax.ShapeDtypeStruct((ROWS, DM), BF16),
        in_specs=[
            pl.BlockSpec(memory_space=vmem),
            pl.BlockSpec(memory_space=pltpu.SMEM),
            pl.BlockSpec(memory_space=pltpu.SMEM),
            pl.BlockSpec(memory_space=pl.ANY),
            pl.BlockSpec(memory_space=pl.ANY),
        ],
        out_specs=pl.BlockSpec(memory_space=vmem),
        scratch_shapes=[
            vmem((DM, FF), BF16),
            vmem((FF, DM), BF16),
            vmem((GA, NZ, 16, WA // 2), BF16),
            vmem((GROUPS, SLAB, WA), BF16),
            vmem((GROUPS, SLAB, WA + 128), BF16),
            vmem((KB, NY, YR, WB), F32),
            vmem((TOKENS, TOKENS), BF16),
            vmem((KB, NY, YR, WB), BF16),
            vmem((KB, NY, YR, WB), BF16),
            vmem((KB, YR, WB), F32),
            vmem((KB, YR, WB), BF16),
            vmem((KB, YR, WB), BF16),
            vmem((KB, NY, YR, WB), BF16),
            vmem((NC, TOKENS // NC, DM), F32),
            vmem((JD, TOKENS // NC, WD), BF16),
            vmem((JD, TOKENS // NC, WD), BF16),
            vmem((JD, NX, SLAB, WD), BF16),
            vmem((JD, NX, SLAB, WD), BF16),
            vmem((JD, NX, SLAB, WD), F32),
            vmem((JD, NZ, 16, WD // 2), BF16),
            vmem((JD, NZ, 16, WD // 2), BF16),
            dma((2,)),
            dma((GA, NZ)), dma((GA, NZ)),
            dma((GA, NX)), dma((GA, NX)),
            dma((GA, NX)), dma((GA, NX)),
            dma((KB, NY)), dma((KB, NY)),
            dma((KB,)), dma((KB,)),
            dma((KB, NY)), dma((KB, NY)),
            dma((JD,)), dma((JD,)),
            dma((JD, NX)), dma((JD, NX)),
            dma((JD, NZ)), dma((JD, NZ)),
        ],
        compiler_params=pltpu.CompilerParams(
            collective_id=0, has_side_effects=True, vmem_limit_bytes=48 << 20
        ),
    )(tokens, partner, spans, up_weight, down_weight)


def solution(mesh):
    placed = (
        P("wide", "narrow"),
        P("narrow", "wide"),
        P("wide", "narrow"),
        P("wide"),
        P("wide", None),
    )
    return jax.shard_map(
        body, mesh=mesh, in_specs=placed, out_specs=P("wide", "narrow"), check_vma=False
    )
```

time: 630 us -> 87.6 us (0.14)
  blocking collectives: 294 us -> 0 us
  waiting for transfers between devices: 247 us -> 0 us
  Pallas kernels: 0 us -> 81.4 us
  starting transfers between devices: 47 us -> 0 us
  between operations: 15.7 us -> 0.01 us
  local copies, waits for them, and re-layouts: 16 us -> 5.99 us
    unnamed x1 -> x0, blocking collectives: 234 us -> none
    all_gather x1 -> x0, waiting for transfers between devices: 128 us -> none  [body(): gathered = lax.all_gather(tokens, 'wide', axis=0, tiled=True)]
    reduce_scatter x1 -> x0, waiting for transfers between devices: 116 us -> none  [body(): lax.psum_scatter(jnp.dot(gathered, up_weight, preferred_element_type=jnp....]
    pallas_call x0 -> x1, Pallas kernels: none -> 81.4 us  [body(): pl.pallas_call(kernel, out_shape=jax.ShapeDtypeStruct((ROWS, DM), BF16),...]
    all_gather x1 -> x0, blocking collectives: 59.9 us -> none  [body(): hidden = lax.all_gather(hidden_part, 'narrow', axis=0, tiled=True)]
    unnamed x16 -> x0, starting transfers between devices: 41.7 us -> none
    unnamed x29 -> x11, local copies, waits for them, and re-layouts: 14.8 us -> 5.99 us
  transfers between devices with their start and end apart: 20 -> 0, of which waited for: 3 -> 0; matrix products, arithmetic and copies ran while one was open for 1% -> 0% of each run, Pallas kernels for 0% -> 0%
where the time goes in v1:
time: 87.6 us; the launch traced here: 87.4 us
  Pallas kernels  81.4 us (93%)
  local copies, waits for them, and re-layouts  5.99 us (7%)
    pallas_call x1, Pallas kernels, body(): pl.pallas_call(kernel, out_shape=jax.ShapeDtypeStruct((ROWS, DM), BF16),...  81.4 us
    unnamed x11, local copies, waits for them, and re-layouts  5.99 us

profile of v1, /device:TPU:1, one launch (start us, length us, event | category | flops | bytes accessed | tf_op | source)
XLA Modules:
  0.0 87.4 jit_solution(4459402885530877782)
XLA Ops:
  0.0 0.0 copy-start
  0.0 1.7 %copy-done = bf16[1536,768]{1,0:T(8,128)(2,1)S(1)} copy-done((bf16[1536,768]{1,0:T(8,128)(2,1)S(1)}, bf16[1536,768]{1,0:T(8,128)(2,1)}, u32[]{:S(2)}) %copy-start) | copy-done | bytes 2359320
  1.7 0.0 copy-start.1
  1.7 1.7 %copy-done.1 = bf16[768,1536]{1,0:T(8,128)(2,1)S(1)} copy-done((bf16[768,1536]{1,0:T(8,128)(2,1)S(1)}, bf16[768,1536]{1,0:T(8,128)(2,1)}, u32[]{:S(2)}) %copy-start.1) | copy-done | bytes 2359320
  3.3 0.0 copy-start.2
  3.3 0.7 copy-done.2
  4.1 0.0 copy-start.3
  4.1 0.7 copy-done.3
  4.7 0.0 copy-start.4
  4.7 0.7 copy-done.4
  5.4 81.4 %shard_map.55 = bf16[6,1536]{1,0:T(8,128)(2,1)S(1)} custom-call(bf16[6,1536]{1,0:T(8,128)(2,1)S(1)} %copy-done.2, s32[6]{0:T(128)S(1)} %copy-done.3, s32[1,2]{1,0:T(1,128)S(1)} %copy-done.4, bf16[1536,768]{1,0:T(8,128)(2,1)S(1)} %copy-done, bf16[768,1536]{1,0:T(8,128)(2,1)S(1)} %copy-done.1), custom_call_target="tpu_custom_call" | custom-call | tf_op jit(solution)/shard_map/pallas_call | solution.py:271
  86.8 0.6 copy.7
Async XLA Ops:
  0.0 1.7 %copy-start = (bf16[1536,768]{1,0:T(8,128)(2,1)S(1)}, bf16[1536,768]{1,0:T(8,128)(2,1)}, u32[]{:S(2)}) copy-start(bf16[1536,768]{1,0:T(8,128)(2,1)} %up_hbm.1) | copy-start | bytes 7077892
  1.7 1.7 %copy-start.1 = (bf16[768,1536]{1,0:T(8,128)(2,1)S(1)}, bf16[768,1536]{1,0:T(8,128)(2,1)}, u32[]{:S(2)}) copy-start(bf16[768,1536]{1,0:T(8,128)(2,1)} %down_hbm.1) | copy-start | bytes 7077892
  3.3 0.7 copy-start.2
  4.1 0.7 copy-start.3
  4.7 0.7 copy-start.4

commit v2 on v1

v2 whole, which is shorter than its diff:
```python
import jax
import jax.numpy as jnp
from jax import lax
from jax.experimental import pallas as pl
from jax.experimental.pallas import tpu as pltpu
from jax.sharding import PartitionSpec as P

MESH = pl.DeviceIdType.MESH
BF16 = jnp.bfloat16
F32 = jnp.float32

NZ, NX, NC, NY = 8, 4, 2, 4
ROWS = 6
SLAB = NZ * ROWS
GROUPS = NC * NX
TOKENS = GROUPS * SLAB
DM = 1536
FF = 768
GATED = {"bh": 3}
Z_SEND = (4, 5, 6, 7, 3, 2, 1)
Z_RECV = (1, 2, 3, 4, 5, 6, 7)
KB = 6
WB = FF // KB
YR = TOKENS // NY


def steps(values, size, count):
    total = jnp.zeros_like(values)
    for k in range(1, count):
        total = total + jnp.where(values >= size * k, 1, 0)
    return total


def onehot(condition):
    return jnp.where(condition, 1.0, 0.0).astype(BF16)


def dot(a, b):
    return jnp.dot(a, b, preferred_element_type=F32)


def token_of(place):
    group = steps(place, SLAB, GROUPS)
    inside = place - SLAB * group
    z = steps(inside, ROWS, NZ)
    core = jnp.where(group >= NX, 1, 0)
    block = (z * NX + (group - NX * core)) * NC + core
    return block, ROWS * block + inside - ROWS * z


def kernel(
    tok_hbm, partner_hbm, spans_hbm, up_hbm, down_hbm, out_ref,
    tok_ref, partner_ref, spans_ref, up, down, planes, g, p1, mix, ysend, yrecv, ysum, hsend, hrecv, hid, p2,
    crecv, xsend, xrecv, xown, zsend, zrecv,
    wsem, az_s, az_r, ax_s, ax_r, ac_s, ac_r, by_s, by_r, bh_s, bh_r, cy_s, cy_r,
    dc_s, dc_r, dx_s, dx_r, dz_s, dz_r,
):
    w = lax.axis_index("wide")
    n = lax.axis_index("narrow")
    z, x, c = w // 8, (w // 2) % 4, w % 2
    half, y = n // 4, n % 4

    def z_at(step):
        bits = (z // 4, z // 2 % 2, z % 2)
        flip = (step // 4, step // 2 % 2, step % 2)
        high, middle, low = ((1 - b) if f else b for b, f in zip(bits, flip))
        return 4 * high + 2 * middle + low

    def z_peer(step):
        return ((z_at(step) * NX + x) * NC + c, n)

    def x_peer(d):
        return ((z * NX + (x + d) % NX) * NC + c, n)

    def y_peer(d):
        return (w, half * NY + (y + d) % NY)

    core_peer = ((z * NX + x) * NC + 1 - c, n)
    half_peer = (w, (1 - half) * NY + y)

    def remote(src, dst, send, recv, peer):
        return pltpu.make_async_remote_copy(
            src_ref=src, dst_ref=dst, send_sem=send, recv_sem=recv, device_id=peer, device_id_type=MESH
        )

    sent = []
    flying = {}

    def start(copy, phase=None):
        copy.start()
        if phase in GATED:
            flying[phase][-1].append(copy)
        else:
            sent.append(copy)

    def gate(phase):
        if phase in GATED:
            chunks = flying.setdefault(phase, [])
            if len(chunks) == GATED[phase]:
                for copy in chunks.pop(0):
                    copy.wait_send()
            chunks.append([])

    up_copy = pltpu.make_async_copy(up_hbm, up, wsem.at[0])
    down_copy = pltpu.make_async_copy(down_hbm, down, wsem.at[1])
    tok_copy = pltpu.make_async_copy(tok_hbm, tok_ref, wsem.at[2])
    partner_copy = pltpu.make_async_copy(partner_hbm, partner_ref, wsem.at[3])
    spans_copy = pltpu.make_async_copy(spans_hbm, spans_ref, wsem.at[4])
    tok_copy.start()
    partner_copy.start()
    spans_copy.start()
    up_copy.start()
    down_copy.start()

    barrier = pltpu.get_barrier_semaphore()
    peers = [half_peer]
    peers += [z_peer(d) for d in range(1, NZ)]
    peers += [y_peer(d) for d in range(1, NY)]
    peers += [x_peer(d) for d in range(1, NX)]
    peers += [core_peer]
    for peer in peers:
        pl.semaphore_signal(barrier, inc=1, device_id=peer, device_id_type=MESH)

    tok_copy.wait()
    partner_copy.wait()
    spans_copy.wait()
    tokens = tok_ref[...].astype(F32)
    row = lax.broadcasted_iota(jnp.int32, (ROWS, 128), 0)
    lane = lax.broadcasted_iota(jnp.int32, (ROWS, 128), 1)
    lower = jnp.full((ROWS, 128), spans_ref[0, 0], jnp.int32).astype(F32)
    upper = jnp.full((ROWS, 128), spans_ref[0, 1], jnp.int32).astype(F32)
    place = row.astype(F32)
    relative = jnp.zeros((ROWS, 128), F32)
    for r in range(ROWS):
        value = jnp.full((ROWS, 128), partner_ref[r] - ROWS * (w - 1), jnp.int32).astype(F32)
        relative = jnp.where(row == r, value, relative)
    share = jnp.where(lower > place, 0.5 * (lower - place) / lower, 0.0) + jnp.where(
        upper <= place, 0.5 * (place - upper + 1.0) / (ROWS - upper), 0.0
    )
    info = jnp.where(lane == 0, relative, jnp.where(lane == 1, share, 0.0))
    t10, t11 = tokens[:, 1280:1408], tokens[:, 1408:1536]
    tails = (
        (t10[0:4],),
        (t10[4:6], t11[0:2]),
        (t11[2:6],),
        (info[0:4],),
        (info[4:6], jnp.zeros((2, 128), F32)),
    )
    group = c * NX + x
    for j in range(5):
        main = (tokens[:, j * 128 : (j + 1) * 128], tokens[:, 640 + j * 128 : 768 + j * 128])
        tile = jnp.concatenate(main + tails[j], axis=0)
        planes[group, z, :, j * 128 : (j + 1) * 128] = tile.astype(BF16)

    pl.semaphore_wait(barrier, len(peers))

    def plane(column, step):
        return planes.at[c * NX + column, z_at(step)]

    for step in Z_SEND:
        mine = plane(x, 0)
        start(remote(mine, mine, az_s.at[step], az_r.at[step], z_peer(step)))

    m_at = lax.broadcasted_iota(jnp.int32, (SLAB, NZ * 16), 0)
    q_at = lax.broadcasted_iota(jnp.int32, (SLAB, NZ * 16), 1)
    m_z = steps(m_at, ROWS, NZ)
    m_r = m_at - ROWS * m_z
    q_r = q_at - 16 * m_z
    pick_low = onehot(q_r == m_r)
    pick_high = onehot(q_r == m_r + 6)
    pick_a = onehot((m_r < 4) & (q_r == m_r + 12))
    pick_b = onehot((m_r >= 4) & (q_r == m_r + 8))
    pick_c = onehot((m_r < 2) & (q_r == m_r + 14))
    pick_d = onehot((m_r >= 2) & (q_r == m_r + 10))

    def spread(step):
        if step:
            mine = plane(x, step)
            remote(mine, mine, az_s.at[step], az_r.at[step], z_peer(step)).wait_recv()
        mine = plane(x, step)
        for d in (2, 1, 3):
            start(remote(mine, mine, ax_s.at[step, d], ax_r.at[step, d], x_peer(d)))

    for step in (0, *Z_RECV):
        spread(step)

    for d in (0, 1, 3, 2):
        column = (x + NX - d) % NX
        if d:
            for step in (0, *Z_RECV):
                there = plane(column, step)
                remote(there, there, ax_s.at[step, d], ax_r.at[step, d], x_peer(d)).wait_recv()
        at = c * NX + column
        whole = planes[at].reshape(NZ * 16, 640)
        g[at, :, 0:640] = dot(pick_low, whole).astype(BF16)
        g[at, :, 640:1280] = dot(pick_high, whole).astype(BF16)
        tail = dot(pick_a, whole[:, 0:128]) + dot(pick_b, whole[:, 128:256])
        g[at, :, 1280:1408] = tail.astype(BF16)
        tail = dot(pick_c, whole[:, 128:256]) + dot(pick_d, whole[:, 256:384])
        g[at, :, 1408:1536] = tail.astype(BF16)
        tail = dot(pick_a, whole[:, 384:512]) + dot(pick_b, whole[:, 512:640])
        g[at, :, 1536:1664] = tail.astype(BF16)
        slab = g.at[at]
        start(remote(slab, slab, ac_s.at[d], ac_r.at[d], core_peer))

    up_copy.wait()
    for i in range(2):
        core = c if i == 0 else 1 - c
        if i:
            for d in (0, 1, 3, 2):
                slab = g.at[(1 - c) * NX + (x + NX - d) % NX]
                remote(slab, slab, ac_s.at[d], ac_r.at[d], core_peer).wait_recv()
        a = g[pl.ds(core * NX, NX), :, 0:DM].reshape(TOKENS // NC, DM)
        for k in range(KB):
            part = dot(a, up[:, k * WB : (k + 1) * WB]).reshape(2, YR, WB)
            p1[k, pl.ds(2 * core, 2)] = part
            ysend[k, pl.ds(2 * core, 2)] = part.astype(BF16)
            if i:
                gate("by")
                for d in (2, 1, 3):
                    mine = ysend.at[k, (y + d) % NY]
                    start(remote(mine, yrecv.at[k, d], by_s.at[k, d], by_r.at[k, d], y_peer(d)), "by")

    info = g[:, :, DM : DM + 128].reshape(TOKENS, 128).astype(F32)
    block, _ = token_of(lax.broadcasted_iota(jnp.int32, (TOKENS, 1), 0))
    partner = (ROWS * (block - 1)).astype(F32) + info[:, 0:1]
    share = info[:, 1:2]
    _, token = token_of(lax.broadcasted_iota(jnp.int32, (1, TOKENS), 1))
    at = lax.broadcasted_iota(jnp.int32, (TOKENS, TOKENS), 0)
    to = lax.broadcasted_iota(jnp.int32, (TOKENS, TOKENS), 1)
    matrix = jnp.where(at == to, 1.0 - share, 0.0) + jnp.where(token.astype(F32) == partner, share, 0.0)
    mix[...] = matrix.astype(BF16).reshape(NC, TOKENS // NC, TOKENS)

    for k in range(KB):
        total = p1[k, y]
        for d in (1, 3, 2):
            remote(yrecv.at[k, d], yrecv.at[k, d], by_s.at[k, d], by_r.at[k, d], y_peer(d)).wait_recv()
            total = total + yrecv[k, d].astype(F32)
        ysum[k] = total
        hsend[k] = total.astype(BF16)
        gate("bh")
        start(remote(hsend.at[k], hrecv.at[k], bh_s.at[k], bh_r.at[k], half_peer), "bh")
    for k in range(KB):
        remote(hsend.at[k], hrecv.at[k], bh_s.at[k], bh_r.at[k], half_peer).wait_recv()
        preact = ysum[k] + hrecv[k].astype(F32)
        hid[k, y] = jax.nn.gelu(preact, approximate=True).astype(BF16)
        mine = hid.at[k, y]
        gate("cy")
        for d in (2, 1, 3):
            start(remote(mine, mine, cy_s.at[k, d], cy_r.at[k, d], y_peer(d)), "cy")

    down_copy.wait()
    for k in range(KB):
        for d in (1, 3, 2):
            slot = hid.at[k, (y + NY - d) % NY]
            remote(slot, slot, cy_s.at[k, d], cy_r.at[k, d], y_peer(d)).wait_recv()
        hidden = hid[k].reshape(TOKENS, WB)
        rows = pl.ds(k * WB, WB)
        if k < KB - 1:
            hidden = dot(mix[...].reshape(TOKENS, TOKENS), hidden).astype(BF16)
            part = dot(hidden, down[rows, :]).reshape(p2.shape)
            p2[...] = part if k == 0 else part + p2[...]
        else:
            for core in (1 - c, c):
                part = dot(dot(mix[core], hidden).astype(BF16), down[rows, :])
                p2[core] = p2[core] + part.reshape(NX, 2, SLAB // 2, DM)
                if core is not c:
                    for far in (1, 0):
                        mine = p2.at[1 - c, :, z_at(4 * far) // 4]
                        start(remote(mine, crecv.at[far], dc_s.at[far], dc_r.at[far], core_peer))

    p_at = lax.broadcasted_iota(jnp.int32, (NX * 64, NX * SLAB // 2), 0)
    s_at = lax.broadcasted_iota(jnp.int32, (NX * 64, NX * SLAB // 2), 1)
    p_block = steps(p_at, 16, NX * 4)
    p_row = p_at - 16 * p_block
    s_row = s_at - ROWS * p_block
    put_low = onehot((p_row < 6) & (s_row == p_row))
    put_high = onehot((p_row >= 6) & (p_row < 12) & (s_row == p_row - 6))
    put_a = onehot((p_row >= 12) & (s_row == p_row - 12))
    put_b = onehot((p_row >= 12) & (p_row < 14) & (s_row == p_row - 8))
    put_c = onehot((p_row >= 14) & (s_row == p_row - 14))
    put_d = onehot((p_row >= 12) & (s_row == p_row - 10))

    def packed(rows, j):
        tile = dot(put_low, rows[:, j * 128 : (j + 1) * 128])
        tile = tile + dot(put_high, rows[:, 640 + j * 128 : 768 + j * 128])
        t10, t11 = rows[:, 1280:1408], rows[:, 1408:1536]
        if j == 0:
            tile = tile + dot(put_a, t10)
        if j == 1:
            tile = tile + dot(put_b, t10) + dot(put_c, t11)
        if j == 2:
            tile = tile + dot(put_d, t11)
        return tile.reshape(NX, 4, 16, 128)

    order = ((7, 6, 5, 4), (3, 2, 1, 0))
    for far in (1, 0):
        mine = p2.at[1 - c, :, z_at(4 * far) // 4]
        remote(mine, crecv.at[far], dc_s.at[far], dc_r.at[far], core_peer).wait_recv()
        total = (p2[c, :, z_at(4 * far) // 4] + crecv[far]).reshape(NX * SLAB // 2, DM)
        first = total.astype(BF16)
        for j in range(5):
            xsend[far, :, :, :, j * 128 : (j + 1) * 128] = packed(first, j).astype(BF16)
        for step in order[1 - far]:
            for d in (2, 1, 3):
                mine = xsend.at[far, (x + d) % NX, z_at(step) % 4]
                start(remote(mine, xrecv.at[step, d], dx_s.at[step, d], dx_r.at[step, d], x_peer(d)))
        rest = (total - first.astype(F32)).astype(BF16)
        for j in range(5):
            xown[far, :, :, :, j * 128 : (j + 1) * 128] = packed(rest, j)
    for step in (*order[0], *order[1]):
        far, at = step // 4, z_at(step) % 4
        total = xown[far, x, at] + xsend[far, x, at].astype(F32)
        for d in (1, 3, 2):
            there = xrecv.at[step, d]
            remote(there, there, dx_s.at[step, d], dx_r.at[step, d], x_peer(d)).wait_recv()
            total = total + xrecv[step, d].astype(F32)
        if step:
            zsend[step] = total.astype(BF16)
            start(remote(zsend.at[step], zrecv.at[step], dz_s.at[step], dz_r.at[step], z_peer(step)))
    for step in (1, 2, 3, 4, 5, 6, 7):
        remote(zsend.at[step], zrecv.at[step], dz_s.at[step], dz_r.at[step], z_peer(step)).wait_recv()
        total = total + zrecv[step].astype(F32)
    for j in range(5):
        tile = total[:, j * 128 : (j + 1) * 128]
        out_ref[:, j * 128 : (j + 1) * 128] = tile[0:6].astype(BF16)
        out_ref[:, 640 + j * 128 : 768 + j * 128] = tile[6:12].astype(BF16)
    t10 = (total[12:16, 0:128], total[12:14, 128:256])
    t11 = (total[14:16, 128:256], total[12:16, 256:384])
    out_ref[:, 1280:1408] = jnp.concatenate(t10, axis=0).astype(BF16)
    out_ref[:, 1408:1536] = jnp.concatenate(t11, axis=0).astype(BF16)

    for chunks in ([sent], *flying.values()):
        for copies in chunks:
            for copy in copies:
                copy.wait_send()


def body(tokens, up_weight, down_weight, partner, spans):
    dma = pltpu.SemaphoreType.DMA
    vmem = pltpu.VMEM
    return pl.pallas_call(
        kernel,
        out_shape=jax.ShapeDtypeStruct((ROWS, DM), BF16),
        in_specs=[pl.BlockSpec(memory_space=pltpu.HBM)] * 5,
        out_specs=pl.BlockSpec(memory_space=vmem),
        scratch_shapes=[
            vmem((ROWS, DM), BF16),
            pltpu.SMEM((ROWS,), jnp.int32),
            pltpu.SMEM((1, 2), jnp.int32),
            vmem((DM, FF), BF16),
            vmem((FF, DM), BF16),
            vmem((GROUPS, NZ, 16, 640), BF16),
            vmem((GROUPS, SLAB, DM + 128), BF16),
            vmem((KB, NY, YR, WB), F32),
            vmem((NC, TOKENS // NC, TOKENS), BF16),
            vmem((KB, NY, YR, WB), BF16),
            vmem((KB, NY, YR, WB), BF16),
            vmem((KB, YR, WB), F32),
            vmem((KB, YR, WB), BF16),
            vmem((KB, YR, WB), BF16),
            vmem((KB, NY, YR, WB), BF16),
            vmem((NC, NX, 2, SLAB // 2, DM), F32),
            vmem((2, NX, SLAB // 2, DM), F32),
            vmem((2, NX, 4, 16, 640), BF16),
            vmem((NZ, NX, 16, 640), BF16),
            vmem((2, NX, 4, 16, 640), F32),
            vmem((NZ, 16, 640), BF16),
            vmem((NZ, 16, 640), BF16),
            dma((5,)),
            dma((NZ,)), dma((NZ,)),
            dma((NZ, NX)), dma((NZ, NX)),
            dma((NX,)), dma((NX,)),
            dma((KB, NY)), dma((KB, NY)),
            dma((KB,)), dma((KB,)),
            dma((KB, NY)), dma((KB, NY)),
            dma((2,)), dma((2,)),
            dma((NZ, NX)), dma((NZ, NX)),
            dma((NZ,)), dma((NZ,)),
        ],
        compiler_params=pltpu.CompilerParams(
            collective_id=0, has_side_effects=True, vmem_limit_bytes=60 << 20
        ),
    )(tokens, partner, spans, up_weight, down_weight)


def solution(mesh):
    placed = (
        P("wide", "narrow"),
        P("narrow", "wide"),
        P("wide", "narrow"),
        P("wide"),
        P("wide", None),
    )
    return jax.shard_map(
        body, mesh=mesh, in_specs=placed, out_specs=P("wide", "narrow"), check_vma=False
    )
```

time: 87.6 us -> 77.7 us (0.89)
  Pallas kernels: 81.4 us -> 76.2 us
  local copies, waits for them, and re-layouts: 5.99 us -> 1.35 us
    pallas_call x1, Pallas kernels: 81.4 us -> 76.2 us  [body(): pl.pallas_call(kernel, out_shape=jax.ShapeDtypeStruct((ROWS, DM), BF16),...]
    unnamed x11 -> x1, local copies, waits for them, and re-layouts: 5.99 us -> 1.35 us
where the time goes in v2:
time: 77.7 us; the launch traced here: 77.5 us
  Pallas kernels  76.2 us (98%)
  local copies, waits for them, and re-layouts  1.35 us (2%)
    pallas_call x1, Pallas kernels, body(): pl.pallas_call(kernel, out_shape=jax.ShapeDtypeStruct((ROWS, DM), BF16),...  76.2 us

profile of v2, /device:TPU:1, one launch (start us, length us, event | category | flops | bytes accessed | tf_op | source)
XLA Modules:
  0.0 77.5 jit_solution(10639549634782718766)
XLA Ops:
  0.0 76.2 %shard_map.55 = bf16[6,1536]{1,0:T(8,128)(2,1)} custom-call(bf16[6,1536]{1,0:T(8,128)(2,1)} %tok_hbm.1, s32[6]{0:T(128)} %partner_hbm.1, s32[1,2]{1,0:T(1,128)} %spans_hbm.1, bf16[1536,768]{1,0:T(8,128)(2,1)} %up_hbm.1, bf16[768,1536]{1,0:T(8,128)(2,1)} %down_hbm.1), custom_call_target="tpu_custom_call" | custom-call | tf_op jit(solution)/shard_map/pallas_call | solution.py:342
  76.2 1.3 %copy.7 = bf16[6,1536]{1,0:T(8,128)(2,1)} copy(bf16[6,1536]{1,0:T(8,128)(2,1)} %shard_map.55) | data formatting | bytes 36864

commit v3 on v2

--- a/solution.py
+++ b/solution.py
@@ -11,17 +11,18 @@
 
 NZ, NX, NC, NY = 8, 4, 2, 4
 ROWS = 6
-SLAB = NZ * ROWS
-GROUPS = NC * NX
-TOKENS = GROUPS * SLAB
+SLAB = NZ // 2 * ROWS
+PART = NX * SLAB
+HALF = NC * PART
+TOKENS = 2 * HALF
 DM = 1536
 FF = 768
-GATED = {"bh": 3}
-Z_SEND = (4, 5, 6, 7, 3, 2, 1)
-Z_RECV = (1, 2, 3, 4, 5, 6, 7)
-KB = 6
+GATED = {}
+EARLY = 4
+Z_SEND = (1, 2, 3, 4, 5, 6, 7)
+KB = 3
 WB = FF // KB
-YR = TOKENS // NY
+YR = HALF // NY
 
 
 def steps(values, size, count):
@@ -39,13 +40,16 @@
     return jnp.dot(a, b, preferred_element_type=F32)
 
 
-def token_of(place):
-    group = steps(place, SLAB, GROUPS)
+def token_of(place, z_high):
+    group = steps(place, SLAB, TOKENS // SLAB)
     inside = place - SLAB * group
-    z = steps(inside, ROWS, NZ)
-    core = jnp.where(group >= NX, 1, 0)
-    block = (z * NX + (group - NX * core)) * NC + core
-    return block, ROWS * block + inside - ROWS * z
+    low = steps(inside, ROWS, NZ // 2)
+    far = jnp.where(group >= NC * NX, 1, 0)
+    core = jnp.where(group - NC * NX * far >= NX, 1, 0)
+    column = group - NC * NX * far - NX * core
+    z = (NZ // 2) * (z_high + far - 2 * z_high * far) + low
+    block = (z * NX + column) * NC + core
+    return block, ROWS * block + inside - ROWS * low
 
 
 def kernel(
@@ -146,26 +150,32 @@
         (info[0:4],),
         (info[4:6], jnp.zeros((2, 128), F32)),
     )
-    group = c * NX + x
     for j in range(5):
         main = (tokens[:, j * 128 : (j + 1) * 128], tokens[:, 640 + j * 128 : 768 + j * 128])
         tile = jnp.concatenate(main + tails[j], axis=0)
-        planes[group, z, :, j * 128 : (j + 1) * 128] = tile.astype(BF16)
+        planes[0, c, x, z % 4, :, j * 128 : (j + 1) * 128] = tile.astype(BF16)
 
     pl.semaphore_wait(barrier, len(peers))
 
     def plane(column, step):
-        return planes.at[c * NX + column, z_at(step)]
+        return planes.at[step // 4, c, column, z_at(step) % 4]
 
     for step in Z_SEND:
-        mine = plane(x, 0)
-        start(remote(mine, mine, az_s.at[step], az_r.at[step], z_peer(step)))
-
-    m_at = lax.broadcasted_iota(jnp.int32, (SLAB, NZ * 16), 0)
-    q_at = lax.broadcasted_iota(jnp.int32, (SLAB, NZ * 16), 1)
-    m_z = steps(m_at, ROWS, NZ)
-    m_r = m_at - ROWS * m_z
-    q_r = q_at - 16 * m_z
+        there = planes.at[step // 4, c, x, z % 4]
+        start(remote(plane(x, 0), there, az_s.at[step], az_r.at[step], z_peer(step)))
+
+    def spread(step):
+        mine = plane(x, step)
+        if step:
+            remote(mine, mine, az_s.at[step], az_r.at[step], z_peer(step)).wait_recv()
+        for d in (2, 1, 3):
+            start(remote(mine, mine, ax_s.at[step, d], ax_r.at[step, d], x_peer(d)))
+
+    m_at = lax.broadcasted_iota(jnp.int32, (PART, PART * 16 // ROWS), 0)
+    q_at = lax.broadcasted_iota(jnp.int32, (PART, PART * 16 // ROWS), 1)
+    m_block = steps(m_at, ROWS, PART // ROWS)
+    m_r = m_at - ROWS * m_block
+    q_r = q_at - 16 * m_block
     pick_low = onehot(q_r == m_r)
     pick_high = onehot(q_r == m_r + 6)
     pick_a = onehot((m_r < 4) & (q_r == m_r + 12))
@@ -173,87 +183,89 @@
     pick_c = onehot((m_r < 2) & (q_r == m_r + 14))
     pick_d = onehot((m_r >= 2) & (q_r == m_r + 10))
 
-    def spread(step):
-        if step:
-            mine = plane(x, step)
-            remote(mine, mine, az_s.at[step], az_r.at[step], z_peer(step)).wait_recv()
-        mine = plane(x, step)
-        for d in (2, 1, 3):
-            start(remote(mine, mine, ax_s.at[step, d], ax_r.at[step, d], x_peer(d)))
-
-    for step in (0, *Z_RECV):
+    def unpack(far):
+        for d in (1, 3, 2):
+            for step in range(4 * far, 4 * far + 4):
+                there = plane((x + NX - d) % NX, step)
+                remote(there, there, ax_s.at[step, d], ax_r.at[step, d], x_peer(d)).wait_recv()
+        whole = planes[far, c].reshape(PART * 16 // ROWS, 640)
+        g[far, c, :, 0:640] = dot(pick_low, whole).astype(BF16)
+        g[far, c, :, 640:1280] = dot(pick_high, whole).astype(BF16)
+        tail = dot(pick_a, whole[:, 0:128]) + dot(pick_b, whole[:, 128:256])
+        g[far, c, :, 1280:1408] = tail.astype(BF16)
+        tail = dot(pick_c, whole[:, 128:256]) + dot(pick_d, whole[:, 256:384])
+        g[far, c, :, 1408:1536] = tail.astype(BF16)
+        tail = dot(pick_a, whole[:, 384:512]) + dot(pick_b, whole[:, 512:640])
+        g[far, c, :, 1536:1664] = tail.astype(BF16)
+        mine = g.at[far, c]
+        start(remote(mine, mine, ac_s.at[far], ac_r.at[far], core_peer))
+
+    def project(far):
+        there = g.at[far, 1 - c]
+        remote(there, there, ac_s.at[far], ac_r.at[far], core_peer).wait_recv()
+        a = g[far, :, :, 0:DM].reshape(HALF, DM)
+        for k in range(KB):
+            part = dot(a, up[:, k * WB : (k + 1) * WB]).reshape(NY, YR, WB)
+            p1[far, k] = part
+            ysend[far, k] = part.astype(BF16)
+            gate("by")
+            for d in (2, 1, 3):
+                mine = ysend.at[far, k, (y + d) % NY]
+                to = yrecv.at[far, k, d]
+                start(remote(mine, to, by_s.at[far, k, d], by_r.at[far, k, d], y_peer(d)), "by")
+
+    def exchange(far):
+        for k in range(KB):
+            total = p1[far, k, y]
+            for d in (1, 3, 2):
+                there = yrecv.at[far, k, d]
+                remote(there, there, by_s.at[far, k, d], by_r.at[far, k, d], y_peer(d)).wait_recv()
+                total = total + yrecv[far, k, d].astype(F32)
+            ysum[far, k] = total
+            hsend[far, k] = total.astype(BF16)
+            gate("bh")
+            mine = hsend.at[far, k]
+            start(remote(mine, hrecv.at[far, k], bh_s.at[far, k], bh_r.at[far, k], half_peer), "bh")
+
+    for step in range(EARLY):
         spread(step)
-
-    for d in (0, 1, 3, 2):
-        column = (x + NX - d) % NX
-        if d:
-            for step in (0, *Z_RECV):
-                there = plane(column, step)
-                remote(there, there, ax_s.at[step, d], ax_r.at[step, d], x_peer(d)).wait_recv()
-        at = c * NX + column
-        whole = planes[at].reshape(NZ * 16, 640)
-        g[at, :, 0:640] = dot(pick_low, whole).astype(BF16)
-        g[at, :, 640:1280] = dot(pick_high, whole).astype(BF16)
-        tail = dot(pick_a, whole[:, 0:128]) + dot(pick_b, whole[:, 128:256])
-        g[at, :, 1280:1408] = tail.astype(BF16)
-        tail = dot(pick_c, whole[:, 128:256]) + dot(pick_d, whole[:, 256:384])
-        g[at, :, 1408:1536] = tail.astype(BF16)
-        tail = dot(pick_a, whole[:, 384:512]) + dot(pick_b, whole[:, 512:640])
-        g[at, :, 1536:1664] = tail.astype(BF16)
-        slab = g.at[at]
-        start(remote(slab, slab, ac_s.at[d], ac_r.at[d], core_peer))
-
+    unpack(0)
+    for step in range(EARLY, NZ):
+        spread(step)
     up_copy.wait()
-    for i in range(2):
-        core = c if i == 0 else 1 - c
-        if i:
-            for d in (0, 1, 3, 2):
-                slab = g.at[(1 - c) * NX + (x + NX - d) % NX]
-                remote(slab, slab, ac_s.at[d], ac_r.at[d], core_peer).wait_recv()
-        a = g[pl.ds(core * NX, NX), :, 0:DM].reshape(TOKENS // NC, DM)
-        for k in range(KB):
-            part = dot(a, up[:, k * WB : (k + 1) * WB]).reshape(2, YR, WB)
-            p1[k, pl.ds(2 * core, 2)] = part
-            ysend[k, pl.ds(2 * core, 2)] = part.astype(BF16)
-            if i:
-                gate("by")
-                for d in (2, 1, 3):
-                    mine = ysend.at[k, (y + d) % NY]
-                    start(remote(mine, yrecv.at[k, d], by_s.at[k, d], by_r.at[k, d], y_peer(d)), "by")
-
-    info = g[:, :, DM : DM + 128].reshape(TOKENS, 128).astype(F32)
-    block, _ = token_of(lax.broadcasted_iota(jnp.int32, (TOKENS, 1), 0))
+    project(0)
+    unpack(1)
+    exchange(0)
+    project(1)
+
+    info = g[:, :, :, DM : DM + 128].reshape(TOKENS, 128).astype(F32)
+    block, _ = token_of(lax.broadcasted_iota(jnp.int32, (TOKENS, 1), 0), z // 4)
     partner = (ROWS * (block - 1)).astype(F32) + info[:, 0:1]
     share = info[:, 1:2]
-    _, token = token_of(lax.broadcasted_iota(jnp.int32, (1, TOKENS), 1))
+    _, token = token_of(lax.broadcasted_iota(jnp.int32, (1, TOKENS), 1), z // 4)
     at = lax.broadcasted_iota(jnp.int32, (TOKENS, TOKENS), 0)
     to = lax.broadcasted_iota(jnp.int32, (TOKENS, TOKENS), 1)
     matrix = jnp.where(at == to, 1.0 - share, 0.0) + jnp.where(token.astype(F32) == partner, share, 0.0)
-    mix[...] = matrix.astype(BF16).reshape(NC, TOKENS // NC, TOKENS)
-
-    for k in range(KB):
-        total = p1[k, y]
-        for d in (1, 3, 2):
-            remote(yrecv.at[k, d], yrecv.at[k, d], by_s.at[k, d], by_r.at[k, d], y_peer(d)).wait_recv()
-            total = total + yrecv[k, d].astype(F32)
-        ysum[k] = total
-        hsend[k] = total.astype(BF16)
-        gate("bh")
-        start(remote(hsend.at[k], hrecv.at[k], bh_s.at[k], bh_r.at[k], half_peer), "bh")
-    for k in range(KB):
-        remote(hsend.at[k], hrecv.at[k], bh_s.at[k], bh_r.at[k], half_peer).wait_recv()
-        preact = ysum[k] + hrecv[k].astype(F32)
-        hid[k, y] = jax.nn.gelu(preact, approximate=True).astype(BF16)
-        mine = hid.at[k, y]
-        gate("cy")
-        for d in (2, 1, 3):
-            start(remote(mine, mine, cy_s.at[k, d], cy_r.at[k, d], y_peer(d)), "cy")
+    mix[...] = matrix.astype(BF16).reshape(mix.shape)
+
+    exchange(1)
+    for far in range(2):
+        for k in range(KB):
+            there = hrecv.at[far, k]
+            remote(there, there, bh_s.at[far, k], bh_r.at[far, k], half_peer).wait_recv()
+            preact = ysum[far, k] + hrecv[far, k].astype(F32)
+            hid[k, far, y] = jax.nn.gelu(preact, approximate=True).astype(BF16)
+            mine = hid.at[k, far, y]
+            gate("cy")
+            for d in (2, 1, 3):
+                start(remote(mine, mine, cy_s.at[far, k, d], cy_r.at[far, k, d], y_peer(d)), "cy")
 
     down_copy.wait()
     for k in range(KB):
-        for d in (1, 3, 2):
-            slot = hid.at[k, (y + NY - d) % NY]
-            remote(slot, slot, cy_s.at[k, d], cy_r.at[k, d], y_peer(d)).wait_recv()
+        for far in range(2):
+            for d in (1, 3, 2):
+                there = hid.at[k, far, (y + NY - d) % NY]
+                remote(there, there, cy_s.at[far, k, d], cy_r.at[far, k, d], y_peer(d)).wait_recv()
         hidden = hid[k].reshape(TOKENS, WB)
         rows = pl.ds(k * WB, WB)
         if k < KB - 1:
@@ -262,15 +274,16 @@
             p2[...] = part if k == 0 else part + p2[...]
         else:
             for core in (1 - c, c):
-                part = dot(dot(mix[core], hidden).astype(BF16), down[rows, :])
-                p2[core] = p2[core] + part.reshape(NX, 2, SLAB // 2, DM)
+                mixed = dot(mix[:, core].reshape(HALF, TOKENS), hidden).astype(BF16)
+                part = dot(mixed, down[rows, :])
+                p2[:, core] = p2[:, core] + part.reshape(2, NX, SLAB, DM)
                 if core is not c:
                     for far in (1, 0):
-                        mine = p2.at[1 - c, :, z_at(4 * far) // 4]
+                        mine = p2.at[far, 1 - c]
                         start(remote(mine, crecv.at[far], dc_s.at[far], dc_r.at[far], core_peer))
 
-    p_at = lax.broadcasted_iota(jnp.int32, (NX * 64, NX * SLAB // 2), 0)
-    s_at = lax.broadcasted_iota(jnp.int32, (NX * 64, NX * SLAB // 2), 1)
+    p_at = lax.broadcasted_iota(jnp.int32, (NX * 64, PART), 0)
+    s_at = lax.broadcasted_iota(jnp.int32, (NX * 64, PART), 1)
     p_block = steps(p_at, 16, NX * 4)
     p_row = p_at - 16 * p_block
     s_row = s_at - ROWS * p_block
@@ -295,9 +308,9 @@
 
     order = ((7, 6, 5, 4), (3, 2, 1, 0))
     for far in (1, 0):
-        mine = p2.at[1 - c, :, z_at(4 * far) // 4]
+        mine = p2.at[far, 1 - c]
         remote(mine, crecv.at[far], dc_s.at[far], dc_r.at[far], core_peer).wait_recv()
-        total = (p2[c, :, z_at(4 * far) // 4] + crecv[far]).reshape(NX * SLAB // 2, DM)
+        total = (p2[far, c] + crecv[far]).reshape(PART, DM)
         first = total.astype(BF16)
         for j in range(5):
             xsend[far, :, :, :, j * 128 : (j + 1) * 128] = packed(first, j).astype(BF16)
@@ -350,18 +363,18 @@
             pltpu.SMEM((1, 2), jnp.int32),
             vmem((DM, FF), BF16),
             vmem((FF, DM), BF16),
-            vmem((GROUPS, NZ, 16, 640), BF16),
-            vmem((GROUPS, SLAB, DM + 128), BF16),
-            vmem((KB, NY, YR, WB), F32),
-            vmem((NC, TOKENS // NC, TOKENS), BF16),
-            vmem((KB, NY, YR, WB), BF16),
-            vmem((KB, NY, YR, WB), BF16),
-            vmem((KB, YR, WB), F32),
-            vmem((KB, YR, WB), BF16),
-            vmem((KB, YR, WB), BF16),
-            vmem((KB, NY, YR, WB), BF16),
-            vmem((NC, NX, 2, SLAB // 2, DM), F32),
-            vmem((2, NX, SLAB // 2, DM), F32),
+            vmem((2, NC, NX, NZ // 2, 16, 640), BF16),
+            vmem((2, NC, PART, DM + 128), BF16),
+            vmem((2, KB, NY, YR, WB), F32),
+            vmem((2, NC, PART, TOKENS), BF16),
+            vmem((2, KB, NY, YR, WB), BF16),
+            vmem((2, KB, NY, YR, WB), BF16),
+            vmem((2, KB, YR, WB), F32),
+            vmem((2, KB, YR, WB), BF16),
+            vmem((2, KB, YR, WB), BF16),
+            vmem((KB, 2, NY, YR, WB), BF16),
+            vmem((2, NC, NX, SLAB, DM), F32),
+            vmem((2, NX, SLAB, DM), F32),
             vmem((2, NX, 4, 16, 640), BF16),
             vmem((NZ, NX, 16, 640), BF16),
             vmem((2, NX, 4, 16, 640), F32),
@@ -370,10 +383,10 @@
             dma((5,)),
             dma((NZ,)), dma((NZ,)),
             dma((NZ, NX)), dma((NZ, NX)),
-            dma((NX,)), dma((NX,)),
-            dma((KB, NY)), dma((KB, NY)),
-            dma((KB,)), dma((KB,)),
-            dma((KB, NY)), dma((KB, NY)),
+            dma((2,)), dma((2,)),
+            dma((2, KB, NY)), dma((2, KB, NY)),
+            dma((2, KB)), dma((2, KB)),
+            dma((2, KB, NY)), dma((2, KB, NY)),
             dma((2,)), dma((2,)),
             dma((NZ, NX)), dma((NZ, NX)),
             dma((NZ,)), dma((NZ,)),

time: 77.7 us -> 72.9 us (0.938)
  Pallas kernels: 76.2 us -> 71.3 us
    pallas_call x1, Pallas kernels: 76.2 us -> 71.3 us  [body(): pl.pallas_call(kernel, out_shape=jax.ShapeDtypeStruct((ROWS, DM), BF16),...]
where the time goes in v3:
time: 72.9 us; the launch traced here: 72.7 us
  Pallas kernels  71.3 us (98%)
  local copies, waits for them, and re-layouts  1.35 us (2%)
    pallas_call x1, Pallas kernels, body(): pl.pallas_call(kernel, out_shape=jax.ShapeDtypeStruct((ROWS, DM), BF16),...  71.3 us

profile of v3, /device:TPU:1, one launch (start us, length us, event | category | flops | bytes accessed | tf_op | source)
XLA Modules:
  0.0 72.7 jit_solution(4648128207148571897)
XLA Ops:
  0.0 71.3 %shard_map.55 = bf16[6,1536]{1,0:T(8,128)(2,1)} custom-call(bf16[6,1536]{1,0:T(8,128)(2,1)} %tok_hbm.1, s32[6]{0:T(128)} %partner_hbm.1, s32[1,2]{1,0:T(1,128)} %spans_hbm.1, bf16[1536,768]{1,0:T(8,128)(2,1)} %up_hbm.1, bf16[768,1536]{1,0:T(8,128)(2,1)} %down_hbm.1), custom_call_target="tpu_custom_call" | custom-call | tf_op jit(solution)/shard_map/pallas_call | solution.py:355
  71.3 1.3 %copy.7 = bf16[6,1536]{1,0:T(8,128)(2,1)} copy(bf16[6,1536]{1,0:T(8,128)(2,1)} %shard_map.55) | data formatting | bytes 36864

commit v4 on v3

--- a/solution.py
+++ b/solution.py
@@ -176,12 +176,17 @@
     m_block = steps(m_at, ROWS, PART // ROWS)
     m_r = m_at - ROWS * m_block
     q_r = q_at - 16 * m_block
-    pick_low = onehot(q_r == m_r)
-    pick_high = onehot(q_r == m_r + 6)
-    pick_a = onehot((m_r < 4) & (q_r == m_r + 12))
-    pick_b = onehot((m_r >= 4) & (q_r == m_r + 8))
-    pick_c = onehot((m_r < 2) & (q_r == m_r + 14))
-    pick_d = onehot((m_r >= 2) & (q_r == m_r + 10))
+    picks = jnp.concatenate(
+        (
+            onehot(q_r == m_r),
+            onehot(q_r == m_r + 6),
+            onehot((m_r < 4) & (q_r == m_r + 12)),
+            onehot((m_r >= 4) & (q_r == m_r + 8)),
+            onehot((m_r < 2) & (q_r == m_r + 14)),
+            onehot((m_r >= 2) & (q_r == m_r + 10)),
+        ),
+        axis=0,
+    )
 
     def unpack(far):
         for d in (1, 3, 2):
@@ -189,14 +194,12 @@
                 there = plane((x + NX - d) % NX, step)
                 remote(there, there, ax_s.at[step, d], ax_r.at[step, d], x_peer(d)).wait_recv()
         whole = planes[far, c].reshape(PART * 16 // ROWS, 640)
-        g[far, c, :, 0:640] = dot(pick_low, whole).astype(BF16)
-        g[far, c, :, 640:1280] = dot(pick_high, whole).astype(BF16)
-        tail = dot(pick_a, whole[:, 0:128]) + dot(pick_b, whole[:, 128:256])
-        g[far, c, :, 1280:1408] = tail.astype(BF16)
-        tail = dot(pick_c, whole[:, 128:256]) + dot(pick_d, whole[:, 256:384])
-        g[far, c, :, 1408:1536] = tail.astype(BF16)
-        tail = dot(pick_a, whole[:, 384:512]) + dot(pick_b, whole[:, 512:640])
-        g[far, c, :, 1536:1664] = tail.astype(BF16)
+        low, high, first, second, third, fourth = dot(picks, whole).reshape(6, PART, 640)
+        g[far, c, :, 0:640] = low.astype(BF16)
+        g[far, c, :, 640:1280] = high.astype(BF16)
+        g[far, c, :, 1280:1408] = (first[:, 0:128] + second[:, 128:256]).astype(BF16)
+        g[far, c, :, 1408:1536] = (third[:, 128:256] + fourth[:, 256:384]).astype(BF16)
+        g[far, c, :, 1536:1664] = (first[:, 384:512] + second[:, 512:640]).astype(BF16)
         mine = g.at[far, c]
         start(remote(mine, mine, ac_s.at[far], ac_r.at[far], core_peer))
 
@@ -282,45 +285,51 @@
                         mine = p2.at[far, 1 - c]
                         start(remote(mine, crecv.at[far], dc_s.at[far], dc_r.at[far], core_peer))
 
-    p_at = lax.broadcasted_iota(jnp.int32, (NX * 64, PART), 0)
-    s_at = lax.broadcasted_iota(jnp.int32, (NX * 64, PART), 1)
+    p_at = lax.broadcasted_iota(jnp.int32, (NX * 64, 2 * PART), 0)
+    s_at = lax.broadcasted_iota(jnp.int32, (NX * 64, 2 * PART), 1)
     p_block = steps(p_at, 16, NX * 4)
     p_row = p_at - 16 * p_block
-    s_row = s_at - ROWS * p_block
-    put_low = onehot((p_row < 6) & (s_row == p_row))
-    put_high = onehot((p_row >= 6) & (p_row < 12) & (s_row == p_row - 6))
-    put_a = onehot((p_row >= 12) & (s_row == p_row - 12))
-    put_b = onehot((p_row >= 12) & (p_row < 14) & (s_row == p_row - 8))
-    put_c = onehot((p_row >= 14) & (s_row == p_row - 14))
-    put_d = onehot((p_row >= 12) & (s_row == p_row - 10))
-
-    def packed(rows, j):
-        tile = dot(put_low, rows[:, j * 128 : (j + 1) * 128])
-        tile = tile + dot(put_high, rows[:, 640 + j * 128 : 768 + j * 128])
+    one = s_at < PART
+    two = s_at >= PART
+    s_row = s_at - PART * jnp.where(two, 1, 0) - ROWS * p_block
+    inside = (s_row >= 0) & (s_row < ROWS)
+    put_main = onehot(inside & ((one & (s_row == p_row)) | (two & (s_row == p_row - 6))))
+    put_middle = onehot(
+        inside & ((one & (p_row < 14) & (s_row == p_row - 8)) | (two & (s_row == p_row - 14)))
+    )
+    put_middle = jnp.where(p_row >= 12, put_middle, 0)
+    put_first = onehot(inside & (p_row >= 12) & (s_row == p_row - 12))[:, 0:PART]
+    put_last = onehot(inside & (p_row >= 12) & (s_row == p_row - 10))[:, 0:PART]
+
+    def pack(rows, to):
+        main = dot(put_main, jnp.concatenate((rows[:, 0:640], rows[:, 640:1280]), axis=0))
         t10, t11 = rows[:, 1280:1408], rows[:, 1408:1536]
-        if j == 0:
-            tile = tile + dot(put_a, t10)
-        if j == 1:
-            tile = tile + dot(put_b, t10) + dot(put_c, t11)
-        if j == 2:
-            tile = tile + dot(put_d, t11)
-        return tile.reshape(NX, 4, 16, 128)
-
+        tails = (
+            dot(put_first, t10),
+            dot(put_middle, jnp.concatenate((t10, t11), axis=0)),
+            dot(put_last, t11),
+        )
+        for j in range(5):
+            tile = main[:, j * 128 : (j + 1) * 128]
+            if j < 3:
+                tile = tile + tails[j]
+            to[:, :, :, j * 128 : (j + 1) * 128] = tile.reshape(NX, 4, 16, 128).astype(to.dtype)
+
+    rests = []
     order = ((7, 6, 5, 4), (3, 2, 1, 0))
     for far in (1, 0):
         mine = p2.at[far, 1 - c]
         remote(mine, crecv.at[far], dc_s.at[far], dc_r.at[far], core_peer).wait_recv()
         total = (p2[far, c] + crecv[far]).reshape(PART, DM)
         first = total.astype(BF16)
-        for j in range(5):
-            xsend[far, :, :, :, j * 128 : (j + 1) * 128] = packed(first, j).astype(BF16)
+        pack(first, xsend.at[far])
         for step in order[1 - far]:
             for d in (2, 1, 3):
                 mine = xsend.at[far, (x + d) % NX, z_at(step) % 4]
                 start(remote(mine, xrecv.at[step, d], dx_s.at[step, d], dx_r.at[step, d], x_peer(d)))
-        rest = (total - first.astype(F32)).astype(BF16)
-        for j in range(5):
-            xown[far, :, :, :, j * 128 : (j + 1) * 128] = packed(rest, j)
+        rests.append((far, (total - first.astype(F32)).astype(BF16)))
+    for far, rest in rests:
+        pack(rest, xown.at[far])
     for step in (*order[0], *order[1]):
         far, at = step // 4, z_at(step) % 4
         total = xown[far, x, at] + xsend[far, x, at].astype(F32)

time: 72.9 us -> 72.7 us (level)
  no operation moved by 1% of the time
where the time goes in v4:
time: 72.7 us; the launch traced here: 72.5 us
  Pallas kernels  71.2 us (98%)
  local copies, waits for them, and re-layouts  1.35 us (2%)
    pallas_call x1, Pallas kernels, body(): pl.pallas_call(kernel, out_shape=jax.ShapeDtypeStruct((ROWS, DM), BF16),...  71.2 us

profile of v4, /device:TPU:1, one launch (start us, length us, event | category | flops | bytes accessed | tf_op | source)
XLA Modules:
  0.0 72.5 jit_solution(2492921729224706389)
XLA Ops:
  0.0 71.2 %shard_map.55 = bf16[6,1536]{1,0:T(8,128)(2,1)} custom-call(bf16[6,1536]{1,0:T(8,128)(2,1)} %tok_hbm.1, s32[6]{0:T(128)} %partner_hbm.1, s32[1,2]{1,0:T(1,128)} %spans_hbm.1, bf16[1536,768]{1,0:T(8,128)(2,1)} %up_hbm.1, bf16[768,1536]{1,0:T(8,128)(2,1)} %down_hbm.1), custom_call_target="tpu_custom_call" | custom-call | tf_op jit(solution)/shard_map/pallas_call | solution.py:364
  71.2 1.3 %copy.7 = bf16[6,1536]{1,0:T(8,128)(2,1)} copy(bf16[6,1536]{1,0:T(8,128)(2,1)} %shard_map.55) | data formatting | bytes 36864

commit v5 on v4

--- a/solution.py
+++ b/solution.py
@@ -276,14 +276,13 @@
             part = dot(hidden, down[rows, :]).reshape(p2.shape)
             p2[...] = part if k == 0 else part + p2[...]
         else:
-            for core in (1 - c, c):
-                mixed = dot(mix[:, core].reshape(HALF, TOKENS), hidden).astype(BF16)
+            for core, far in ((1 - c, 1), (1 - c, 0), (c, 1), (c, 0)):
+                mixed = dot(mix[far, core], hidden).astype(BF16)
                 part = dot(mixed, down[rows, :])
-                p2[:, core] = p2[:, core] + part.reshape(2, NX, SLAB, DM)
+                p2[far, core] = p2[far, core] + part.reshape(NX, SLAB, DM)
                 if core is not c:
-                    for far in (1, 0):
-                        mine = p2.at[far, 1 - c]
-                        start(remote(mine, crecv.at[far], dc_s.at[far], dc_r.at[far], core_peer))
+                    mine = p2.at[far, 1 - c]
+                    start(remote(mine, crecv.at[far], dc_s.at[far], dc_r.at[far], core_peer))
 
     p_at = lax.broadcasted_iota(jnp.int32, (NX * 64, 2 * PART), 0)
     s_at = lax.broadcasted_iota(jnp.int32, (NX * 64, 2 * PART), 1)

time: 72.7 us -> 72.9 us (level)
  no operation moved by 1% of the time
where the time goes in v5:
time: 72.9 us; the launch traced here: 72.7 us
  Pallas kernels  71.4 us (98%)
  local copies, waits for them, and re-layouts  1.35 us (2%)
    pallas_call x1, Pallas kernels, body(): pl.pallas_call(kernel, out_shape=jax.ShapeDtypeStruct((ROWS, DM), BF16),...  71.4 us

profile of v5, /device:TPU:1, one launch (start us, length us, event | category | flops | bytes accessed | tf_op | source)
XLA Modules:
  0.0 72.7 jit_solution(204865345361097830)
XLA Ops:
  0.0 71.4 %shard_map.55 = bf16[6,1536]{1,0:T(8,128)(2,1)} custom-call(bf16[6,1536]{1,0:T(8,128)(2,1)} %tok_hbm.1, s32[6]{0:T(128)} %partner_hbm.1, s32[1,2]{1,0:T(1,128)} %spans_hbm.1, bf16[1536,768]{1,0:T(8,128)(2,1)} %up_hbm.1, bf16[768,1536]{1,0:T(8,128)(2,1)} %down_hbm.1), custom_call_target="tpu_custom_call" | custom-call | tf_op jit(solution)/shard_map/pallas_call | solution.py:363
  71.4 1.3 %copy.7 = bf16[6,1536]{1,0:T(8,128)(2,1)} copy(bf16[6,1536]{1,0:T(8,128)(2,1)} %shard_map.55) | data formatting | bytes 36864
